TPU v7x, 512 devices: a whole 4x8x8 slice. The times are simulated.
512 devices in a mesh: fsdp: 32 (over y, z_lo), col: 16 (over x, z_hi, core).
Axes of the slice: x: 4, y: 8, z: 8 (z_hi: 2, z_lo: 4; z = z_hi * 4 + z_lo), core: 2. Of those that a mesh axis runs over, the one named last changes fastest.
Arguments:
- joined_gradient: bfloat16 [6144, 18432], P('fsdp', 'col'), may hold values from -6 to 6
- output_gradient: bfloat16 [6144, 6144], P('fsdp', 'col'), may hold values from -6 to 6
- joined_left_basis: bfloat16 [6144, 512], P('fsdp', 'col'), may hold values from -0.078125 to 0.078125
- joined_right_basis: bfloat16 [18432, 512], P('col', 'fsdp'), may hold values from -0.046875 to 0.046875
- output_left_basis: bfloat16 [6144, 512], P('fsdp', 'col'), may hold values from -0.078125 to 0.078125
- output_right_basis: bfloat16 [6144, 512], P('col', 'fsdp'), may hold values from -0.078125 to 0.078125
- joined_left_eigen: float32 [512], replicated, may hold values from 0.05 to 20
- joined_right_eigen: float32 [512], replicated, may hold values from 0.05 to 20
- output_left_eigen: float32 [512], replicated, may hold values from 0.05 to 20
- output_right_eigen: float32 [512], replicated, may hold values from 0.05 to 20
- damping: float32 [1], replicated, may hold values from 0.5 to 1
Outputs:
- joined_update: float32 [6144, 18432], P('fsdp', 'col')
- output_update: float32 [6144, 6144], P('fsdp', 'col')
All inputs are finite; a program needn't handle non-finite values.
Results may differ from a plain program's by a relative error of at most 0.0003.
Values may be sent and summed in bfloat16 or wider, within the bound.
No kernel may reach another device: no remote copies, remote signals or barrier semaphores. Data moves between devices by JAX's collectives and lax.ppermute only.
A program may use at most 64 MiB of HBM per device.

v0:
```python
import jax
import jax.numpy as jnp
from jax import lax
from jax.sharding import Mesh, PartitionSpec as P

FSDP = ("yp", "yb", "zp", "zb")
COL = ("x", "zh", "c")
QUAD = ("yb", "zb")
OCT = ("yp", "zp")
ROUND = (8, 7)


def shifted(eigen, damp):
    return 1.0 / (eigen + damp) - 1.0 / damp


def exchange(blocks, axes):
    return lax.all_to_all(blocks, axes, 0, 0, tiled=True)


def halves(wide):
    high = lax.reduce_precision(wide, *ROUND)
    return (high.astype(jnp.bfloat16), (wide - high).astype(jnp.bfloat16))


def dot_wide_left(wide, narrow, dims):
    high, low = halves(wide)
    dot = lambda part: lax.dot_general(
        part, narrow, (dims, ((), ())), preferred_element_type=jnp.float32
    )
    return dot(high) + dot(low)


def dot_wide_right(narrow, wide, dims):
    high, low = halves(wide)
    dot = lambda part: lax.dot_general(
        narrow, part, (dims, ((), ())), preferred_element_type=jnp.float32
    )
    return dot(high) + dot(low)


def pack(values):
    top = jnp.max(jnp.abs(values), axis=-2, keepdims=True)
    power = jnp.clip(jnp.floor(jnp.log2(jnp.maximum(top, 1e-30))), -100.0, 120.0)
    scaled = (values * jnp.exp2(14.0 - power)).astype(jnp.float16)
    tail = jnp.broadcast_to(power.astype(jnp.float16), values.shape[:-2] + (8, values.shape[-1]))
    return jnp.concatenate([scaled, tail], axis=-2)


def unpack(packed):
    rows = packed.shape[-2] - 8
    power = packed[..., rows : rows + 1, :].astype(jnp.float32)
    return packed[..., :rows, :].astype(jnp.float32) * jnp.exp2(power - 14.0)


def spread(values, count):
    return jnp.broadcast_to(values[None], (count,) + values.shape)


def swap(values, axis):
    return lax.ppermute(values, axis, [(0, 1), (1, 0)])


def core_part(values, core, own):
    half = values.shape[0] // 2
    return lax.dynamic_slice_in_dim(values, (core if own else 1 - core) * half, half, 0)


def local(
    joined_gradient,
    output_gradient,
    joined_left_basis,
    joined_right_basis,
    output_left_basis,
    output_right_basis,
    joined_left_eigen,
    joined_right_eigen,
    output_left_eigen,
    output_right_eigen,
    damping,
):
    damp = damping[0]
    quad = lax.axis_index("yb") * 2 + lax.axis_index("zb")
    level = lax.axis_index("yp")
    core = lax.axis_index("c")
    is_output = quad == 3
    left_shift = shifted(jnp.where(is_output, output_left_eigen, joined_left_eigen), damp)
    right_shift = shifted(jnp.where(is_output, output_right_eigen, joined_right_eigen), damp)
    left_shift = left_shift.reshape(4, 2, 2, 32).transpose(2, 0, 1, 3)
    left_shift = jnp.where(lax.axis_index("zh") == 1, left_shift[:, :, ::-1], left_shift).reshape(
        512
    )
    own_shift = lax.dynamic_slice_in_dim(left_shift, level * 128, 128, 0)
    right_shift = right_shift.reshape(4, 2, 2, 2, 16).transpose(2, 0, 1, 3, 4)
    right_shift = jnp.where(lax.axis_index("zp") == 1, right_shift[::-1], right_shift).reshape(512)
    right = jnp.concatenate([joined_right_basis.T, output_right_basis.T], axis=1)
    lefts = [
        jnp.concatenate([basis.T[:16], basis.T[16:]], axis=1)
        for basis in (joined_left_basis, output_left_basis)
    ]
    left = jnp.concatenate(lefts, axis=0)
    other = swap(left, "zh")
    lefts = [
        jnp.concatenate([left[rows], other[rows]], axis=0) for rows in (slice(0, 16), slice(16, 32))
    ]
    lefts = (lefts[0], lefts[0], lefts[0], lefts[1])
    gradients = (
        joined_gradient[:, :384],
        joined_gradient[:, 384:768],
        joined_gradient[:, 768:],
        output_gradient,
    )
    sent = jnp.stack(
        [
            jnp.concatenate([gradients[j], right[:, 384 * j : 384 * j + 384], lefts[j]], axis=0)
            for j in range(4)
        ]
    )
    got = exchange(sent, QUAD)
    gradient = got[:, :192].reshape(768, 384)
    left = got[:, 208:].reshape(4, 2, 16, 384)
    left = jnp.stack([left[..., :192], left[..., 192:]], axis=2).reshape(4, 64, 192)
    left = jnp.concatenate([left[0], left[1], left[2], left[3]], axis=1)
    left = exchange(spread(left, 4), "x").reshape(256, 768)
    left = lax.all_gather(left, "c", axis=0, tiled=True)
    right = got[:, 192:208].reshape(64, 384)
    scaled = (right.astype(jnp.float32) * 2.0**19).astype(jnp.float16)
    rows = jnp.dot(left, gradient, preferred_element_type=jnp.float32)
    rows = jnp.concatenate([pack(rows.reshape(4, 128, 384)), spread(scaled, 4)], axis=1)
    got = exchange(rows, "yp")
    rows = jnp.sum(unpack(got[:, :136]), axis=0)
    rows = (rows + unpack(swap(pack(rows), "zp"))) * own_shift[:, None]
    rows = unpack(exchange(spread(pack(rows), 4), "yp")).reshape(512, 384)
    right = (got[:, 136:].reshape(256, 384).astype(jnp.float32) * 2.0 ** (-19)).astype(jnp.bfloat16)
    right = jnp.concatenate([right, swap(right, "zp")], axis=0)
    lifted = dot_wide_right(left, rows, ((0,), (0,)))
    applied = gradient.astype(jnp.float32) / damp + lifted
    cols = dot_wide_left(applied, right, ((1,), (1,)))
    cols = core_part(cols, core, True) + swap(core_part(cols, core, False), "c")
    cols = jnp.sum(unpack(exchange(pack(cols.reshape(4, 96, 512)), "x")), axis=0)
    cols = cols + unpack(swap(pack(cols), "zh"))
    cols = unpack(exchange(spread(pack(cols), 4), QUAD))
    same = (lax.broadcasted_iota(jnp.int32, (4, 1, 1), 0) == 3) == is_output
    cols = jnp.sum(jnp.where(same, cols, 0.0), axis=0)
    cols = exchange(spread(pack(cols), 4), "x")
    cols = unpack(lax.all_gather(cols, "c", axis=0, tiled=True)).reshape(768, 512)
    update = lifted / damp + dot_wide_left(cols * right_shift[None, :], right, ((1,), (0,)))
    update = unpack(exchange(pack(update.reshape(4, 192, 384)), QUAD))
    joined_update = (
        jnp.concatenate([update[0], update[1], update[2]], axis=1)
        + joined_gradient.astype(jnp.float32) / damp / damp
    )
    output_update = update[3] + output_gradient.astype(jnp.float32) / damp / damp
    return (joined_update, output_update)


def solution(mesh):
    fine = Mesh(mesh.devices.reshape(4, 2, 2, 2, 4, 2, 2), ("yp", "yb", "zp", "zb", "x", "zh", "c"))
    placed = (
        P(FSDP, COL),
        P(FSDP, COL),
        P(FSDP, COL),
        P(COL, FSDP),
        P(FSDP, COL),
        P(COL, FSDP),
        P(),
        P(),
        P(),
        P(),
        P(),
    )
    return jax.shard_map(
        local, mesh=fine, in_specs=placed, out_specs=(P(FSDP, COL), P(FSDP, COL)), check_vma=False
    )
```

profile of v0, /device:TPU:1, one launch (start us, length us, event | category | flops | bytes accessed | tf_op | source)
XLA Modules:
  0.0 173.8 jit_solution(16419256087640813020)
XLA Ops:
  0.6 0.8 fusion.49
  1.5 11.5 %collective-permute-start = (bf16[32,384]{1,0:T(8,128)(2,1)S(1)}, bf16[32,384]{1,0:T(8,128)(2,1)S(1)}, u32[]{:S(2)}, u32[]{:S(2)}) collective-permute-start(bf16[32,384]{1,0:T(8,128)(2,1)S(1)} %maximum_maximum_fusion), channel_id=1, source_target_pairs={{0,2},{2,0},{1,3},{3,1},{4,6},{6,4},{5,7},{7,5},{8,10},{10,8},{9,1... | collective-permute-start | bytes 73736 | tf_op jit(solution)/shard_map/ppermute | solution.py:61
  13.0 1.1 fusion.46
  14.1 0.8 fusion.47
  14.8 0.8 maximum_bitcast_fusion
  15.7 0.1 pad_maximum_fusion
  15.8 11.7 %all_to_all.40 = bf16[4,240,384]{2,1,0:T(8,128)(2,1)S(1)} all-to-all(bf16[4,240,384]{2,1,0:T(8,128)(2,1)S(1)} %pad_maximum_fusion), channel_id=1, replica_groups=mesh['yp'=4,'yb'=2,'zp'=2,'zb'=2,'x'=4,'zh'=2,'c'=2] {'yb','zb'}, dimensions={0} | all-to-all | bytes 1474560 | tf_op jit(solution)/shard_map/all_to_all | solution.py:18
  27.6 0.1 slice_bitcast_fusion.5
  27.7 0.1 pad_maximum_fusion.14
  27.8 0.8 broadcast_in_dim.34
  28.6 4.8 %all-to-all-start.1 = ((bf16[4,64,768]{2,1,0:T(8,128)(2,1)}), bf16[4,64,768]{2,1,0:T(8,128)(2,1)S(1)}, u32[]{:S(2)}, u32[]{:S(2)}) async-start(bf16[4,64,768]{2,1,0:T(8,128)(2,1)} %broadcast_in_dim.34), calls=%async_computation.1 | async-start | bytes 786432 | tf_op jit(solution)/shard_map/all_to_all | solution.py:18
  33.4 6.1 %all-to-all-done.1 = bf16[4,64,768]{2,1,0:T(8,128)(2,1)S(1)} async-done(((bf16[4,64,768]{2,1,0:T(8,128)(2,1)}), bf16[4,64,768]{2,1,0:T(8,128)(2,1)S(1)}, u32[]{:S(2)}, u32[]{:S(2)}) %all-to-all-start.1) | async-done | bytes 393248 | tf_op jit(solution)/shard_map/all_to_all | solution.py:18
  39.6 6.1 %all_gather.6 = bf16[512,768]{1,0:T(8,128)(2,1)S(1)} all-gather(bf16[256,768]{1,0:T(8,128)(2,1)S(1)} %bitcast.98), channel_id=1, replica_groups=mesh['yp'=4,'yb'=2,'zp'=2,'zb'=2,'x'=4,'zh'=2,'c'=2] {'c'}, dimensions={0}, use_global_device_ids=true | all-gather | bytes 1179648 | tf_op jit(solution)/shard_map/all_gather | solution.py:125
  45.7 0.6 abs_reduce_fusion.2
  46.5 1.0 pad_maximum_fusion.1
  47.5 5.9 %all-to-all-start.2 = ((f16[4,200,384]{2,1,0:T(8,128)(2,1)}), f16[4,200,384]{2,1,0:T(8,128)(2,1)S(1)}, u32[]{:S(2)}, u32[]{:S(2)}) async-start(f16[4,200,384]{2,1,0:T(8,128)(2,1)} %pad_maximum_fusion.1), calls=%async_computation.2 | async-start | bytes 1228800 | tf_op jit(solution)/shard_map/all_to_all | solution.py:18
  54.2 0.1 reshape.254
  54.3 14.9 %all-to-all-done.2 = f16[4,200,384]{2,1,0:T(8,128)(2,1)S(1)} async-done(((f16[4,200,384]{2,1,0:T(8,128)(2,1)}), f16[4,200,384]{2,1,0:T(8,128)(2,1)S(1)}, u32[]{:S(2)}, u32[]{:S(2)}) %all-to-all-start.2) | async-done | bytes 614432 | tf_op jit(solution)/shard_map/all_to_all | solution.py:18
  69.4 4.0 %collective-permute-start.1 = (f16[136,384]{1,0:T(8,128)(2,1)S(1)}, f16[136,384]{1,0:T(8,128)(2,1)S(1)}, u32[]{:S(2)}, u32[]{:S(2)}) collective-permute-start(f16[136,384]{1,0:T(8,128)(2,1)S(1)} %pad_maximum_fusion.12), channel_id=1, source_target_pairs={{0,32},{32,0},{1,33},{33,1},{2,34},{34,2},{3,35},{35,3},{4,36},{36... | collective-permute-start | bytes 313352 | tf_op jit(solution)/shard_map/ppermute | solution.py:61
  73.5 0.1 reshape.255
  73.7 2.1 %collective-permute-done.1 = f16[136,384]{1,0:T(8,128)(2,1)S(1)} collective-permute-done((f16[136,384]{1,0:T(8,128)(2,1)S(1)}, f16[136,384]{1,0:T(8,128)(2,1)S(1)}, u32[]{:S(2)}, u32[]{:S(2)}) %collective-permute-start.1) | collective-permute-done | bytes 104480 | tf_op jit(solution)/shard_map/ppermute | solution.py:61
  75.8 0.1 abs_reduce_fusion.6
  75.9 0.1 multiply_convert_fusion.7
  76.1 0.8 broadcast_in_dim.39
  76.9 8.4 %all-to-all-start.3 = ((f16[4,136,384]{2,1,0:T(8,128)(2,1)}), f16[4,136,384]{2,1,0:T(8,128)(2,1)S(1)}, u32[]{:S(2)}, u32[]{:S(2)}) async-start(f16[4,136,384]{2,1,0:T(8,128)(2,1)} %broadcast_in_dim.39), calls=%async_computation.3 | async-start | bytes 835584 | tf_op jit(solution)/shard_map/all_to_all | solution.py:18
  85.3 1.9 %collective-permute-start.2 = (bf16[256,384]{1,0:T(8,128)(2,1)S(1)}, bf16[256,384]{1,0:T(8,128)(2,1)S(1)}, u32[]{:S(2)}, u32[]{:S(2)}) collective-permute-start(bf16[256,384]{1,0:T(8,128)(2,1)S(1)} %bitcast.92), channel_id=1, source_target_pairs={{0,32},{32,0},{1,33},{33,1},{2,34},{34,2},{3,35},{35,3},{4,36},{36... | collective-permute-start | bytes 589832 | tf_op jit(solution)/shard_map/ppermute | solution.py:61
  87.2 8.0 %all-to-all-done.3 = f16[4,136,384]{2,1,0:T(8,128)(2,1)S(1)} async-done(((f16[4,136,384]{2,1,0:T(8,128)(2,1)}), f16[4,136,384]{2,1,0:T(8,128)(2,1)S(1)}, u32[]{:S(2)}, u32[]{:S(2)}) %all-to-all-start.3) | async-done | bytes 417824 | tf_op jit(solution)/shard_map/all_to_all | solution.py:18
  95.3 0.1 fusion.3
  95.4 0.6 fusion.51
  96.0 1.6 divide_add_fusion
  97.7 1.1 collective-permute-done.2
  98.8 0.6 fusion.4
  99.4 0.6 convolution_add_fusion
  100.1 4.5 %collective-permute-start.3 = (f32[384,512]{1,0:T(8,128)S(1)}, f32[384,512]{1,0:T(8,128)S(1)}, u32[]{:S(2)}, u32[]{:S(2)}) collective-permute-start(f32[384,512]{1,0:T(8,128)S(1)} %constant_dynamic-slice_fusion), channel_id=1, source_target_pairs={{0,1},{1,0},{2,3},{3,2},{4,5},{5,4},{6,7},{7,6},{8,9},{9,8},{10,11... | collective-permute-start | bytes 2359304 | tf_op jit(solution)/shard_map/ppermute | solution.py:61
  104.6 1.9 %collective-permute-done.3 = f32[384,512]{1,0:T(8,128)S(1)} collective-permute-done((f32[384,512]{1,0:T(8,128)S(1)}, f32[384,512]{1,0:T(8,128)S(1)}, u32[]{:S(2)}, u32[]{:S(2)}) %collective-permute-start.3) | collective-permute-done | bytes 786464 | tf_op jit(solution)/shard_map/ppermute | solution.py:61
  106.5 0.1 dynamic-slice_add_fusion
  106.8 0.1 multiply_convert_fusion.1
  106.9 0.1 pad_maximum_fusion.3
  107.0 10.4 %all_to_all.41 = f16[4,104,512]{2,1,0:T(8,128)(2,1)S(1)} all-to-all(f16[4,104,512]{2,1,0:T(8,128)(2,1)S(1)} %pad_maximum_fusion.3), channel_id=1, replica_groups=mesh['yp'=4,'yb'=2,'zp'=2,'zb'=2,'x'=4,'zh'=2,'c'=2] {'x'}, dimensions={0} | all-to-all | bytes 851968 | tf_op jit(solution)/shard_map/all_to_all | solution.py:18
  117.6 6.8 %collective-permute-start.4 = (f16[104,512]{1,0:T(8,128)(2,1)S(1)}, f16[104,512]{1,0:T(8,128)(2,1)S(1)}, u32[]{:S(2)}, u32[]{:S(2)}) collective-permute-start(f16[104,512]{1,0:T(8,128)(2,1)S(1)} %pad_maximum_fusion.9), channel_id=1, source_target_pairs={{0,2},{2,0},{1,3},{3,1},{4,6},{6,4},{5,7},{7,5},{8,10},{10,8},{9,1... | collective-permute-start | bytes 319496 | tf_op jit(solution)/shard_map/ppermute | solution.py:61
  124.5 2.6 %collective-permute-done.4 = f16[104,512]{1,0:T(8,128)(2,1)S(1)} collective-permute-done((f16[104,512]{1,0:T(8,128)(2,1)S(1)}, f16[104,512]{1,0:T(8,128)(2,1)S(1)}, u32[]{:S(2)}, u32[]{:S(2)}) %collective-permute-start.4) | collective-permute-done | bytes 106528 | tf_op jit(solution)/shard_map/ppermute | solution.py:61
  127.3 0.8 broadcast_in_dim.44
  128.1 3.5 %all-to-all-start.5 = ((f16[4,104,512]{2,1,0:T(8,128)(2,1)}), f16[4,104,512]{2,1,0:T(8,128)(2,1)S(1)}, u32[]{:S(2)}, u32[]{:S(2)}) async-start(f16[4,104,512]{2,1,0:T(8,128)(2,1)} %broadcast_in_dim.44), calls=%async_computation.5 | async-start | bytes 851968 | tf_op jit(solution)/shard_map/all_to_all | solution.py:18
  131.6 4.9 %all-to-all-done.5 = f16[4,104,512]{2,1,0:T(8,128)(2,1)S(1)} async-done(((f16[4,104,512]{2,1,0:T(8,128)(2,1)}), f16[4,104,512]{2,1,0:T(8,128)(2,1)S(1)}, u32[]{:S(2)}, u32[]{:S(2)}) %all-to-all-start.5) | async-done | bytes 426016 | tf_op jit(solution)/shard_map/all_to_all | solution.py:18
  136.4 0.1 select_reduce_fusion
  136.7 0.8 broadcast_in_dim.51
  137.5 3.5 %all-to-all-start.6 = ((f16[4,104,512]{2,1,0:T(8,128)(2,1)}), f16[4,104,512]{2,1,0:T(8,128)(2,1)S(1)}, u32[]{:S(2)}, u32[]{:S(2)}) async-start(f16[4,104,512]{2,1,0:T(8,128)(2,1)} %broadcast_in_dim.51), calls=%async_computation.6 | async-start | bytes 851968 | tf_op jit(solution)/shard_map/all_to_all | solution.py:18
  141.0 0.1 reshape.259
  141.1 0.1 mul.237
  141.2 6.2 %all-to-all-done.6 = f16[4,104,512]{2,1,0:T(8,128)(2,1)S(1)} async-done(((f16[4,104,512]{2,1,0:T(8,128)(2,1)}), f16[4,104,512]{2,1,0:T(8,128)(2,1)S(1)}, u32[]{:S(2)}, u32[]{:S(2)}) %all-to-all-start.6) | async-done | bytes 426016 | tf_op jit(solution)/shard_map/all_to_all | solution.py:18
  147.3 7.9 %all_gather.7 = f16[8,104,512]{2,1,0:T(8,128)(2,1)S(1)} all-gather(f16[4,104,512]{2,1,0:T(8,128)(2,1)S(1)} %all-to-all-done.6), channel_id=1, replica_groups=mesh['yp'=4,'yb'=2,'zp'=2,'zb'=2,'x'=4,'zh'=2,'c'=2] {'c'}, dimensions={0}, use_global_device_ids=true | all-gather | bytes 1277952 | tf_op jit(solution)/shard_map/all_gather | solution.py:146
  155.3 0.2 convert_multiply_fusion
  155.5 0.3 reduce-precision_convert_fusion
  155.8 0.6 fusion.45
  156.4 0.7 copy-done.7
  157.0 0.6 fusion.1
  157.7 0.1 multiply_convert_fusion
  157.9 1.0 pad_maximum_fusion.2
  158.9 3.5 %all-to-all-start.7 = ((f16[4,200,384]{2,1,0:T(8,128)(2,1)}), f16[4,200,384]{2,1,0:T(8,128)(2,1)S(1)}, u32[]{:S(2)}, u32[]{:S(2)}) async-start(f16[4,200,384]{2,1,0:T(8,128)(2,1)} %pad_maximum_fusion.2), calls=%async_computation.7 | async-start | bytes 1228800 | tf_op jit(solution)/shard_map/all_to_all | solution.py:18
  162.4 8.7 %all-to-all-done.7 = f16[4,200,384]{2,1,0:T(8,128)(2,1)S(1)} async-done(((f16[4,200,384]{2,1,0:T(8,128)(2,1)}), f16[4,200,384]{2,1,0:T(8,128)(2,1)S(1)}, u32[]{:S(2)}, u32[]{:S(2)}) %all-to-all-start.7) | async-done | bytes 614432 | tf_op jit(solution)/shard_map/all_to_all | solution.py:18
  171.1 0.1 convert_multiply_fusion.1
  171.3 0.8 copy-done.2
  172.1 0.7 fusion.6
  172.8 1.0 maximum_add_fusion
  (82 shorter events, 1.8 us)
Async XLA Ops:
  0.6 14.2 %copy-start.1 = (bf16[192,384]{1,0:T(8,128)(2,1)S(1)}, bf16[192,384]{1,0:T(8,128)(2,1)}, u32[]{:S(2)}) copy-start(bf16[192,384]{1,0:T(8,128)(2,1)} %param.12) | copy-start | bytes 442372
  1.5 13.3 %collective-permute-start = (bf16[32,384]{1,0:T(8,128)(2,1)S(1)}, bf16[32,384]{1,0:T(8,128)(2,1)S(1)}, u32[]{:S(2)}, u32[]{:S(2)}) collective-permute-start(bf16[32,384]{1,0:T(8,128)(2,1)S(1)} %maximum_maximum_fusion), channel_id=1, source_target_pairs={{0,2},{2,0},{1,3},{3,1},{4,6},{6,4},{5,7},{7,5},{8,10},{10,8},{9,1... | collective-permute-start | bytes 73736 | tf_op jit(solution)/shard_map/ppermute | solution.py:61
  28.6 11.0 %all-to-all-start.1 = ((bf16[4,64,768]{2,1,0:T(8,128)(2,1)}), bf16[4,64,768]{2,1,0:T(8,128)(2,1)S(1)}, u32[]{:S(2)}, u32[]{:S(2)}) async-start(bf16[4,64,768]{2,1,0:T(8,128)(2,1)} %broadcast_in_dim.34), calls=%async_computation.1 | async-start | bytes 786432 | tf_op jit(solution)/shard_map/all_to_all | solution.py:18
  46.4 7.7 %copy-start.3 = (f32[512]{0:T(512)S(1)}, f32[512]{0:T(512)}, u32[]{:S(2)}) copy-start(f32[512]{0:T(512)} %param.20) | copy-start | bytes 6148
  46.4 7.7 %copy-start.4 = (f32[512]{0:T(512)S(1)}, f32[512]{0:T(512)}, u32[]{:S(2)}) copy-start(f32[512]{0:T(512)} %param.18) | copy-start | bytes 6148
  46.5 7.7 %copy-start.5 = (f32[512]{0:T(512)S(1)}, f32[512]{0:T(512)}, u32[]{:S(2)}) copy-start(f32[512]{0:T(512)} %param.19) | copy-start | bytes 6148
  46.5 7.7 %copy-start.6 = (f32[512]{0:T(512)S(1)}, f32[512]{0:T(512)}, u32[]{:S(2)}) copy-start(f32[512]{0:T(512)} %param.17) | copy-start | bytes 6148
  47.5 21.7 %all-to-all-start.2 = ((f16[4,200,384]{2,1,0:T(8,128)(2,1)}), f16[4,200,384]{2,1,0:T(8,128)(2,1)S(1)}, u32[]{:S(2)}, u32[]{:S(2)}) async-start(f16[4,200,384]{2,1,0:T(8,128)(2,1)} %pad_maximum_fusion.1), calls=%async_computation.2 | async-start | bytes 1228800 | tf_op jit(solution)/shard_map/all_to_all | solution.py:18
  69.4 6.3 %collective-permute-start.1 = (f16[136,384]{1,0:T(8,128)(2,1)S(1)}, f16[136,384]{1,0:T(8,128)(2,1)S(1)}, u32[]{:S(2)}, u32[]{:S(2)}) collective-permute-start(f16[136,384]{1,0:T(8,128)(2,1)S(1)} %pad_maximum_fusion.12), channel_id=1, source_target_pairs={{0,32},{32,0},{1,33},{33,1},{2,34},{34,2},{3,35},{35,3},{4,36},{36... | collective-permute-start | bytes 313352 | tf_op jit(solution)/shard_map/ppermute | solution.py:61
  76.9 18.4 %all-to-all-start.3 = ((f16[4,136,384]{2,1,0:T(8,128)(2,1)}), f16[4,136,384]{2,1,0:T(8,128)(2,1)S(1)}, u32[]{:S(2)}, u32[]{:S(2)}) async-start(f16[4,136,384]{2,1,0:T(8,128)(2,1)} %broadcast_in_dim.39), calls=%async_computation.3 | async-start | bytes 835584 | tf_op jit(solution)/shard_map/all_to_all | solution.py:18
  85.3 13.5 %collective-permute-start.2 = (bf16[256,384]{1,0:T(8,128)(2,1)S(1)}, bf16[256,384]{1,0:T(8,128)(2,1)S(1)}, u32[]{:S(2)}, u32[]{:S(2)}) collective-permute-start(bf16[256,384]{1,0:T(8,128)(2,1)S(1)} %bitcast.92), channel_id=1, source_target_pairs={{0,32},{32,0},{1,33},{33,1},{2,34},{34,2},{3,35},{35,3},{4,36},{36... | collective-permute-start | bytes 589832 | tf_op jit(solution)/shard_map/ppermute | solution.py:61
  100.1 6.4 %collective-permute-start.3 = (f32[384,512]{1,0:T(8,128)S(1)}, f32[384,512]{1,0:T(8,128)S(1)}, u32[]{:S(2)}, u32[]{:S(2)}) collective-permute-start(f32[384,512]{1,0:T(8,128)S(1)} %constant_dynamic-slice_fusion), channel_id=1, source_target_pairs={{0,1},{1,0},{2,3},{3,2},{4,5},{5,4},{6,7},{7,6},{8,9},{9,8},{10,11... | collective-permute-start | bytes 2359304 | tf_op jit(solution)/shard_map/ppermute | solution.py:61
  117.6 9.5 %collective-permute-start.4 = (f16[104,512]{1,0:T(8,128)(2,1)S(1)}, f16[104,512]{1,0:T(8,128)(2,1)S(1)}, u32[]{:S(2)}, u32[]{:S(2)}) collective-permute-start(f16[104,512]{1,0:T(8,128)(2,1)S(1)} %pad_maximum_fusion.9), channel_id=1, source_target_pairs={{0,2},{2,0},{1,3},{3,1},{4,6},{6,4},{5,7},{7,5},{8,10},{10,8},{9,1... | collective-permute-start | bytes 319496 | tf_op jit(solution)/shard_map/ppermute | solution.py:61
  128.1 8.3 %all-to-all-start.5 = ((f16[4,104,512]{2,1,0:T(8,128)(2,1)}), f16[4,104,512]{2,1,0:T(8,128)(2,1)S(1)}, u32[]{:S(2)}, u32[]{:S(2)}) async-start(f16[4,104,512]{2,1,0:T(8,128)(2,1)} %broadcast_in_dim.44), calls=%async_computation.5 | async-start | bytes 851968 | tf_op jit(solution)/shard_map/all_to_all | solution.py:18
  137.5 9.8 %all-to-all-start.6 = ((f16[4,104,512]{2,1,0:T(8,128)(2,1)}), f16[4,104,512]{2,1,0:T(8,128)(2,1)S(1)}, u32[]{:S(2)}, u32[]{:S(2)}) async-start(f16[4,104,512]{2,1,0:T(8,128)(2,1)} %broadcast_in_dim.51), calls=%async_computation.6 | async-start | bytes 851968 | tf_op jit(solution)/shard_map/all_to_all | solution.py:18
  155.8 1.3 copy-start.7
  158.9 12.2 %all-to-all-start.7 = ((f16[4,200,384]{2,1,0:T(8,128)(2,1)}), f16[4,200,384]{2,1,0:T(8,128)(2,1)S(1)}, u32[]{:S(2)}, u32[]{:S(2)}) async-start(f16[4,200,384]{2,1,0:T(8,128)(2,1)} %pad_maximum_fusion.2), calls=%async_computation.7 | async-start | bytes 1228800 | tf_op jit(solution)/shard_map/all_to_all | solution.py:18
  171.2 0.9 copy-start.2
  171.2 1.7 copy-start
where the time goes:
time: 175 us; the launch traced here: 174 us
  starting transfers between devices  58.3 us (33%)
  waiting for transfers between devices  56.5 us (32%)
  blocking collectives  36.1 us (21%)
  local copies, waits for them, and re-layouts  8.19 us (5%)
  other arithmetic  7.57 us (4%)
  matrix products  5.23 us (3%)
  between operations  2.01 us (1%)
    all_to_all x6, waiting for transfers between devices, exchange(): return lax.all_to_all(blocks, axes, 0, 0, tiled=True)  48.8 us
    all_to_all x6, starting transfers between devices, exchange(): return lax.all_to_all(blocks, axes, 0, 0, tiled=True)  29.5 us
    ppermute x5, starting transfers between devices, swap(): return lax.ppermute(values, axis, [(0, 1), (1, 0)])  28.8 us
    all_to_all x2, blocking collectives, exchange(): return lax.all_to_all(blocks, axes, 0, 0, tiled=True)  22.1 us
    all_gather x1, blocking collectives, local(): lax.all_gather(cols, 'c', axis=0, tiled=True)  7.88 us
    ppermute x5, waiting for transfers between devices, swap(): return lax.ppermute(values, axis, [(0, 1), (1, 0)])  7.7 us
    all_gather x1, blocking collectives, local(): left = lax.all_gather(left, 'c', axis=0, tiled=True)  6.09 us
  transfers between devices with their start and end apart: 11, of which 10 were waited for; matrix products, arithmetic and copies ran while one was open for 3% of the time, Pallas kernels for 0%

commit v1 on v0

--- a/solution.py
+++ b/solution.py
@@ -143,7 +143,9 @@
     same = (lax.broadcasted_iota(jnp.int32, (4, 1, 1), 0) == 3) == is_output
     cols = jnp.sum(jnp.where(same, cols, 0.0), axis=0)
     cols = exchange(spread(pack(cols), 4), "x")
-    cols = unpack(lax.all_gather(cols, "c", axis=0, tiled=True)).reshape(768, 512)
+    cols = unpack(
+        jnp.concatenate(lax.all_to_all(jnp.stack([cols] * lax.axis_size("c")), "c", 0, 0), axis=0)
+    ).reshape(768, 512)
     update = lifted / damp + dot_wide_left(cols * right_shift[None, :], right, ((1,), (0,)))
     update = unpack(exchange(pack(update.reshape(4, 192, 384)), QUAD))
     joined_update = (

time: 175 us -> 180 us (1.029)
  local copies, waits for them, and re-layouts: 8.19 us -> 11.1 us
  blocking collectives: 36.1 us -> 38.1 us
    all_to_all x0 -> x1, blocking collectives: none -> 9.89 us  [local(): lax.all_to_all(jnp.stack([cols] * lax.axis_size('c')), 'c', 0, 0)]
    all_gather x1 -> x0, blocking collectives: 7.88 us -> none  [local(): lax.all_gather(cols, 'c', axis=0, tiled=True)]
where the time goes in v1:
time: 180 us; the launch traced here: 179 us
  starting transfers between devices  57.9 us (32%)
  waiting for transfers between devices  57 us (32%)
  blocking collectives  38.1 us (21%)
  local copies, waits for them, and re-layouts  11.1 us (6%)
  other arithmetic  7.76 us (4%)
  matrix products  5.19 us (3%)
  between operations  2.02 us (1%)
    all_to_all x6, waiting for transfers between devices, exchange(): return lax.all_to_all(blocks, axes, 0, 0, tiled=True)  48.8 us
    all_to_all x6, starting transfers between devices, exchange(): return lax.all_to_all(blocks, axes, 0, 0, tiled=True)  29.5 us
    ppermute x5, starting transfers between devices, swap(): return lax.ppermute(values, axis, [(0, 1), (1, 0)])  28.5 us
    all_to_all x2, blocking collectives, exchange(): return lax.all_to_all(blocks, axes, 0, 0, tiled=True)  22.1 us
    all_to_all x1, blocking collectives, local(): lax.all_to_all(jnp.stack([cols] * lax.axis_size('c')), 'c', 0, 0)  9.89 us
    ppermute x5, waiting for transfers between devices, swap(): return lax.ppermute(values, axis, [(0, 1), (1, 0)])  8.22 us
    all_gather x1, blocking collectives, local(): left = lax.all_gather(left, 'c', axis=0, tiled=True)  6.09 us
  transfers between devices with their start and end apart: 11, of which 10 were waited for; matrix products, arithmetic and copies ran while one was open for 3% of the time, Pallas kernels for 0%

profile of v1, /device:TPU:1, one launch (start us, length us, event | category | flops | bytes accessed | tf_op | source)
XLA Modules:
  0.0 179.2 jit_solution(17045070501636222841)
XLA Ops:
  0.6 0.8 fusion.49
  1.5 11.5 %collective-permute-start = (bf16[32,384]{1,0:T(8,128)(2,1)S(1)}, bf16[32,384]{1,0:T(8,128)(2,1)S(1)}, u32[]{:S(2)}, u32[]{:S(2)}) collective-permute-start(bf16[32,384]{1,0:T(8,128)(2,1)S(1)} %maximum_maximum_fusion), channel_id=1, source_target_pairs={{0,2},{2,0},{1,3},{3,1},{4,6},{6,4},{5,7},{7,5},{8,10},{10,8},{9,1... | collective-permute-start | bytes 73736 | tf_op jit(solution)/shard_map/ppermute | solution.py:61
  13.0 1.1 fusion.46
  14.1 0.8 fusion.47
  14.8 0.8 maximum_bitcast_fusion
  15.7 0.1 pad_maximum_fusion.1
  15.8 11.7 %all_to_all.45 = bf16[4,240,384]{2,1,0:T(8,128)(2,1)S(1)} all-to-all(bf16[4,240,384]{2,1,0:T(8,128)(2,1)S(1)} %pad_maximum_fusion.1), channel_id=1, replica_groups=mesh['yp'=4,'yb'=2,'zp'=2,'zb'=2,'x'=4,'zh'=2,'c'=2] {'yb','zb'}, dimensions={0} | all-to-all | bytes 1474560 | tf_op jit(solution)/shard_map/all_to_all | solution.py:18
  27.7 0.1 pad_maximum_fusion.15
  27.8 0.8 broadcast_in_dim.34
  28.6 4.8 %all-to-all-start.1 = ((bf16[4,64,768]{2,1,0:T(8,128)(2,1)}), bf16[4,64,768]{2,1,0:T(8,128)(2,1)S(1)}, u32[]{:S(2)}, u32[]{:S(2)}) async-start(bf16[4,64,768]{2,1,0:T(8,128)(2,1)} %broadcast_in_dim.34), calls=%async_computation.1 | async-start | bytes 786432 | tf_op jit(solution)/shard_map/all_to_all | solution.py:18
  33.4 6.1 %all-to-all-done.1 = bf16[4,64,768]{2,1,0:T(8,128)(2,1)S(1)} async-done(((bf16[4,64,768]{2,1,0:T(8,128)(2,1)}), bf16[4,64,768]{2,1,0:T(8,128)(2,1)S(1)}, u32[]{:S(2)}, u32[]{:S(2)}) %all-to-all-start.1) | async-done | bytes 393248 | tf_op jit(solution)/shard_map/all_to_all | solution.py:18
  39.6 6.1 %all_gather.3 = bf16[512,768]{1,0:T(8,128)(2,1)S(1)} all-gather(bf16[256,768]{1,0:T(8,128)(2,1)S(1)} %bitcast.102), channel_id=1, replica_groups=mesh['yp'=4,'yb'=2,'zp'=2,'zb'=2,'x'=4,'zh'=2,'c'=2] {'c'}, dimensions={0}, use_global_device_ids=true | all-gather | bytes 1179648 | tf_op jit(solution)/shard_map/all_gather | solution.py:125
  45.7 0.6 abs_reduce_fusion.2
  46.5 1.0 pad_maximum_fusion.2
  47.5 5.9 %all-to-all-start.2 = ((f16[4,200,384]{2,1,0:T(8,128)(2,1)}), f16[4,200,384]{2,1,0:T(8,128)(2,1)S(1)}, u32[]{:S(2)}, u32[]{:S(2)}) async-start(f16[4,200,384]{2,1,0:T(8,128)(2,1)} %pad_maximum_fusion.2), calls=%async_computation.2 | async-start | bytes 1228800 | tf_op jit(solution)/shard_map/all_to_all | solution.py:18
  54.2 14.9 %all-to-all-done.2 = f16[4,200,384]{2,1,0:T(8,128)(2,1)S(1)} async-done(((f16[4,200,384]{2,1,0:T(8,128)(2,1)}), f16[4,200,384]{2,1,0:T(8,128)(2,1)S(1)}, u32[]{:S(2)}, u32[]{:S(2)}) %all-to-all-start.2) | async-done | bytes 614432 | tf_op jit(solution)/shard_map/all_to_all | solution.py:18
  69.4 4.0 %collective-permute-start.1 = (f16[136,384]{1,0:T(8,128)(2,1)S(1)}, f16[136,384]{1,0:T(8,128)(2,1)S(1)}, u32[]{:S(2)}, u32[]{:S(2)}) collective-permute-start(f16[136,384]{1,0:T(8,128)(2,1)S(1)} %pad_maximum_fusion.13), channel_id=1, source_target_pairs={{0,32},{32,0},{1,33},{33,1},{2,34},{34,2},{3,35},{35,3},{4,36},{36... | collective-permute-start | bytes 313352 | tf_op jit(solution)/shard_map/ppermute | solution.py:61
  73.6 2.1 %collective-permute-done.1 = f16[136,384]{1,0:T(8,128)(2,1)S(1)} collective-permute-done((f16[136,384]{1,0:T(8,128)(2,1)S(1)}, f16[136,384]{1,0:T(8,128)(2,1)S(1)}, u32[]{:S(2)}, u32[]{:S(2)}) %collective-permute-start.1) | collective-permute-done | bytes 104480 | tf_op jit(solution)/shard_map/ppermute | solution.py:61
  75.8 0.1 abs_reduce_fusion.6
  75.9 0.1 multiply_convert_fusion.7
  76.1 0.8 broadcast_in_dim.39
  76.9 8.4 %all-to-all-start.3 = ((f16[4,136,384]{2,1,0:T(8,128)(2,1)}), f16[4,136,384]{2,1,0:T(8,128)(2,1)S(1)}, u32[]{:S(2)}, u32[]{:S(2)}) async-start(f16[4,136,384]{2,1,0:T(8,128)(2,1)} %broadcast_in_dim.39), calls=%async_computation.3 | async-start | bytes 835584 | tf_op jit(solution)/shard_map/all_to_all | solution.py:18
  85.3 1.9 %collective-permute-start.2 = (bf16[256,384]{1,0:T(8,128)(2,1)S(1)}, bf16[256,384]{1,0:T(8,128)(2,1)S(1)}, u32[]{:S(2)}, u32[]{:S(2)}) collective-permute-start(bf16[256,384]{1,0:T(8,128)(2,1)S(1)} %bitcast.95), channel_id=1, source_target_pairs={{0,32},{32,0},{1,33},{33,1},{2,34},{34,2},{3,35},{35,3},{4,36},{36... | collective-permute-start | bytes 589832 | tf_op jit(solution)/shard_map/ppermute | solution.py:61
  87.2 8.0 %all-to-all-done.3 = f16[4,136,384]{2,1,0:T(8,128)(2,1)S(1)} async-done(((f16[4,136,384]{2,1,0:T(8,128)(2,1)}), f16[4,136,384]{2,1,0:T(8,128)(2,1)S(1)}, u32[]{:S(2)}, u32[]{:S(2)}) %all-to-all-start.3) | async-done | bytes 417824 | tf_op jit(solution)/shard_map/all_to_all | solution.py:18
  95.3 0.1 fusion.3
  95.4 0.6 fusion.51
  96.0 1.6 divide_add_fusion
  97.7 1.4 collective-permute-done.2
  99.1 0.6 fusion.4
  99.7 0.6 convolution_add_fusion
  100.3 0.9 constant_dynamic-slice_fusion
  101.2 4.2 %collective-permute-start.3 = (f32[384,512]{1,0:T(8,128)}, f32[384,512]{1,0:T(8,128)S(1)}, u32[]{:S(2)}, u32[]{:S(2)}) collective-permute-start(f32[384,512]{1,0:T(8,128)} %constant_dynamic-slice_fusion), channel_id=1, source_target_pairs={{0,1},{1,0},{2,3},{3,2},{4,5},{5,4},{6,7},{7,6},{8,9},{9,8},{10,11... | collective-permute-start | bytes 2359304 | tf_op jit(solution)/shard_map/ppermute | solution.py:61
  105.5 2.1 %collective-permute-done.3 = f32[384,512]{1,0:T(8,128)S(1)} collective-permute-done((f32[384,512]{1,0:T(8,128)}, f32[384,512]{1,0:T(8,128)S(1)}, u32[]{:S(2)}, u32[]{:S(2)}) %collective-permute-start.3) | collective-permute-done | bytes 786464 | tf_op jit(solution)/shard_map/ppermute | solution.py:61
  107.6 0.1 dynamic-slice_add_fusion
  107.8 0.1 multiply_convert_fusion.1
  107.9 0.1 pad_maximum_fusion.4
  108.0 10.4 %all_to_all.46 = f16[4,104,512]{2,1,0:T(8,128)(2,1)S(1)} all-to-all(f16[4,104,512]{2,1,0:T(8,128)(2,1)S(1)} %pad_maximum_fusion.4), channel_id=1, replica_groups=mesh['yp'=4,'yb'=2,'zp'=2,'zb'=2,'x'=4,'zh'=2,'c'=2] {'x'}, dimensions={0} | all-to-all | bytes 851968 | tf_op jit(solution)/shard_map/all_to_all | solution.py:18
  118.7 6.8 %collective-permute-start.4 = (f16[104,512]{1,0:T(8,128)(2,1)S(1)}, f16[104,512]{1,0:T(8,128)(2,1)S(1)}, u32[]{:S(2)}, u32[]{:S(2)}) collective-permute-start(f16[104,512]{1,0:T(8,128)(2,1)S(1)} %pad_maximum_fusion.10), channel_id=1, source_target_pairs={{0,2},{2,0},{1,3},{3,1},{4,6},{6,4},{5,7},{7,5},{8,10},{10,8},{9,1... | collective-permute-start | bytes 319496 | tf_op jit(solution)/shard_map/ppermute | solution.py:61
  125.5 2.6 %collective-permute-done.4 = f16[104,512]{1,0:T(8,128)(2,1)S(1)} collective-permute-done((f16[104,512]{1,0:T(8,128)(2,1)S(1)}, f16[104,512]{1,0:T(8,128)(2,1)S(1)}, u32[]{:S(2)}, u32[]{:S(2)}) %collective-permute-start.4) | collective-permute-done | bytes 106528 | tf_op jit(solution)/shard_map/ppermute | solution.py:61
  128.3 0.8 broadcast_in_dim.44
  129.1 3.5 %all-to-all-start.5 = ((f16[4,104,512]{2,1,0:T(8,128)(2,1)}), f16[4,104,512]{2,1,0:T(8,128)(2,1)S(1)}, u32[]{:S(2)}, u32[]{:S(2)}) async-start(f16[4,104,512]{2,1,0:T(8,128)(2,1)} %broadcast_in_dim.44), calls=%async_computation.5 | async-start | bytes 851968 | tf_op jit(solution)/shard_map/all_to_all | solution.py:18
  132.6 4.9 %all-to-all-done.5 = f16[4,104,512]{2,1,0:T(8,128)(2,1)S(1)} async-done(((f16[4,104,512]{2,1,0:T(8,128)(2,1)}), f16[4,104,512]{2,1,0:T(8,128)(2,1)S(1)}, u32[]{:S(2)}, u32[]{:S(2)}) %all-to-all-start.5) | async-done | bytes 426016 | tf_op jit(solution)/shard_map/all_to_all | solution.py:18
  137.5 0.1 select_reduce_fusion
  137.8 0.8 broadcast_in_dim.51
  138.6 3.5 %all-to-all-start.6 = ((f16[4,104,512]{2,1,0:T(8,128)(2,1)}), f16[4,104,512]{2,1,0:T(8,128)(2,1)S(1)}, u32[]{:S(2)}, u32[]{:S(2)}) async-start(f16[4,104,512]{2,1,0:T(8,128)(2,1)} %broadcast_in_dim.51), calls=%async_computation.6 | async-start | bytes 851968 | tf_op jit(solution)/shard_map/all_to_all | solution.py:18
  142.2 6.2 %all-to-all-done.6 = f16[4,104,512]{2,1,0:T(8,128)(2,1)S(1)} async-done(((f16[4,104,512]{2,1,0:T(8,128)(2,1)}), f16[4,104,512]{2,1,0:T(8,128)(2,1)S(1)}, u32[]{:S(2)}, u32[]{:S(2)}) %all-to-all-start.6) | async-done | bytes 426016 | tf_op jit(solution)/shard_map/all_to_all | solution.py:18
  148.4 0.2 pad_maximum_fusion
  148.6 0.6 copy.29
  149.1 9.9 %all_to_all.47 = f16[2,4,104,512]{3,1,2,0:T(4,128)(2,1)S(1)} all-to-all(f16[2,4,104,512]{3,1,2,0:T(4,128)(2,1)S(1)} %copy.29), channel_id=1, replica_groups=mesh['yp'=4,'yb'=2,'zp'=2,'zb'=2,'x'=4,'zh'=2,'c'=2] {'c'}, dimensions={0} | all-to-all | bytes 1703936 | tf_op jit(solution)/shard_map/all_to_all | solution.py:147
  159.0 0.3 copy.30
  159.4 0.3 reshape.261
  159.7 0.2 convert_multiply_fusion
  159.9 0.9 copy.31
  160.8 0.3 reduce-precision_convert_fusion
  161.1 0.6 fusion.45
  161.7 0.7 copy-done.7
  162.4 0.6 fusion.1
  163.1 0.1 multiply_convert_fusion
  163.2 1.0 pad_maximum_fusion.3
  164.2 3.5 %all-to-all-start.8 = ((f16[4,200,384]{2,1,0:T(8,128)(2,1)}), f16[4,200,384]{2,1,0:T(8,128)(2,1)S(1)}, u32[]{:S(2)}, u32[]{:S(2)}) async-start(f16[4,200,384]{2,1,0:T(8,128)(2,1)} %pad_maximum_fusion.3), calls=%async_computation.8 | async-start | bytes 1228800 | tf_op jit(solution)/shard_map/all_to_all | solution.py:18
  167.7 8.7 %all-to-all-done.8 = f16[4,200,384]{2,1,0:T(8,128)(2,1)S(1)} async-done(((f16[4,200,384]{2,1,0:T(8,128)(2,1)}), f16[4,200,384]{2,1,0:T(8,128)(2,1)S(1)}, u32[]{:S(2)}, u32[]{:S(2)}) %all-to-all-start.8) | async-done | bytes 614432 | tf_op jit(solution)/shard_map/all_to_all | solution.py:18
  176.6 0.8 copy-done.2
  177.4 0.7 fusion.6
  178.2 1.0 maximum_add_fusion
  (86 shorter events, 2.3 us)
Async XLA Ops:
  0.6 14.2 %copy-start.1 = (bf16[192,384]{1,0:T(8,128)(2,1)S(1)}, bf16[192,384]{1,0:T(8,128)(2,1)}, u32[]{:S(2)}) copy-start(bf16[192,384]{1,0:T(8,128)(2,1)} %param.12) | copy-start | bytes 442372
  1.5 13.3 %collective-permute-start = (bf16[32,384]{1,0:T(8,128)(2,1)S(1)}, bf16[32,384]{1,0:T(8,128)(2,1)S(1)}, u32[]{:S(2)}, u32[]{:S(2)}) collective-permute-start(bf16[32,384]{1,0:T(8,128)(2,1)S(1)} %maximum_maximum_fusion), channel_id=1, source_target_pairs={{0,2},{2,0},{1,3},{3,1},{4,6},{6,4},{5,7},{7,5},{8,10},{10,8},{9,1... | collective-permute-start | bytes 73736 | tf_op jit(solution)/shard_map/ppermute | solution.py:61
  28.6 11.0 %all-to-all-start.1 = ((bf16[4,64,768]{2,1,0:T(8,128)(2,1)}), bf16[4,64,768]{2,1,0:T(8,128)(2,1)S(1)}, u32[]{:S(2)}, u32[]{:S(2)}) async-start(bf16[4,64,768]{2,1,0:T(8,128)(2,1)} %broadcast_in_dim.34), calls=%async_computation.1 | async-start | bytes 786432 | tf_op jit(solution)/shard_map/all_to_all | solution.py:18
  46.4 7.7 %copy-start.3 = (f32[512]{0:T(512)S(1)}, f32[512]{0:T(512)}, u32[]{:S(2)}) copy-start(f32[512]{0:T(512)} %param.20) | copy-start | bytes 6148
  46.4 7.7 %copy-start.4 = (f32[512]{0:T(512)S(1)}, f32[512]{0:T(512)}, u32[]{:S(2)}) copy-start(f32[512]{0:T(512)} %param.18) | copy-start | bytes 6148
  46.5 7.7 %copy-start.5 = (f32[512]{0:T(512)S(1)}, f32[512]{0:T(512)}, u32[]{:S(2)}) copy-start(f32[512]{0:T(512)} %param.19) | copy-start | bytes 6148
  46.5 7.7 %copy-start.6 = (f32[512]{0:T(512)S(1)}, f32[512]{0:T(512)}, u32[]{:S(2)}) copy-start(f32[512]{0:T(512)} %param.17) | copy-start | bytes 6148
  47.5 21.7 %all-to-all-start.2 = ((f16[4,200,384]{2,1,0:T(8,128)(2,1)}), f16[4,200,384]{2,1,0:T(8,128)(2,1)S(1)}, u32[]{:S(2)}, u32[]{:S(2)}) async-start(f16[4,200,384]{2,1,0:T(8,128)(2,1)} %pad_maximum_fusion.2), calls=%async_computation.2 | async-start | bytes 1228800 | tf_op jit(solution)/shard_map/all_to_all | solution.py:18
  69.4 6.3 %collective-permute-start.1 = (f16[136,384]{1,0:T(8,128)(2,1)S(1)}, f16[136,384]{1,0:T(8,128)(2,1)S(1)}, u32[]{:S(2)}, u32[]{:S(2)}) collective-permute-start(f16[136,384]{1,0:T(8,128)(2,1)S(1)} %pad_maximum_fusion.13), channel_id=1, source_target_pairs={{0,32},{32,0},{1,33},{33,1},{2,34},{34,2},{3,35},{35,3},{4,36},{36... | collective-permute-start | bytes 313352 | tf_op jit(solution)/shard_map/ppermute | solution.py:61
  76.9 18.4 %all-to-all-start.3 = ((f16[4,136,384]{2,1,0:T(8,128)(2,1)}), f16[4,136,384]{2,1,0:T(8,128)(2,1)S(1)}, u32[]{:S(2)}, u32[]{:S(2)}) async-start(f16[4,136,384]{2,1,0:T(8,128)(2,1)} %broadcast_in_dim.39), calls=%async_computation.3 | async-start | bytes 835584 | tf_op jit(solution)/shard_map/all_to_all | solution.py:18
  85.3 13.8 %collective-permute-start.2 = (bf16[256,384]{1,0:T(8,128)(2,1)S(1)}, bf16[256,384]{1,0:T(8,128)(2,1)S(1)}, u32[]{:S(2)}, u32[]{:S(2)}) collective-permute-start(bf16[256,384]{1,0:T(8,128)(2,1)S(1)} %bitcast.95), channel_id=1, source_target_pairs={{0,32},{32,0},{1,33},{33,1},{2,34},{34,2},{3,35},{35,3},{4,36},{36... | collective-permute-start | bytes 589832 | tf_op jit(solution)/shard_map/ppermute | solution.py:61
  101.2 6.3 %collective-permute-start.3 = (f32[384,512]{1,0:T(8,128)}, f32[384,512]{1,0:T(8,128)S(1)}, u32[]{:S(2)}, u32[]{:S(2)}) collective-permute-start(f32[384,512]{1,0:T(8,128)} %constant_dynamic-slice_fusion), channel_id=1, source_target_pairs={{0,1},{1,0},{2,3},{3,2},{4,5},{5,4},{6,7},{7,6},{8,9},{9,8},{10,11... | collective-permute-start | bytes 2359304 | tf_op jit(solution)/shard_map/ppermute | solution.py:61
  118.7 9.5 %collective-permute-start.4 = (f16[104,512]{1,0:T(8,128)(2,1)S(1)}, f16[104,512]{1,0:T(8,128)(2,1)S(1)}, u32[]{:S(2)}, u32[]{:S(2)}) collective-permute-start(f16[104,512]{1,0:T(8,128)(2,1)S(1)} %pad_maximum_fusion.10), channel_id=1, source_target_pairs={{0,2},{2,0},{1,3},{3,1},{4,6},{6,4},{5,7},{7,5},{8,10},{10,8},{9,1... | collective-permute-start | bytes 319496 | tf_op jit(solution)/shard_map/ppermute | solution.py:61
  129.1 8.3 %all-to-all-start.5 = ((f16[4,104,512]{2,1,0:T(8,128)(2,1)}), f16[4,104,512]{2,1,0:T(8,128)(2,1)S(1)}, u32[]{:S(2)}, u32[]{:S(2)}) async-start(f16[4,104,512]{2,1,0:T(8,128)(2,1)} %broadcast_in_dim.44), calls=%async_computation.5 | async-start | bytes 851968 | tf_op jit(solution)/shard_map/all_to_all | solution.py:18
  138.6 9.8 %all-to-all-start.6 = ((f16[4,104,512]{2,1,0:T(8,128)(2,1)}), f16[4,104,512]{2,1,0:T(8,128)(2,1)S(1)}, u32[]{:S(2)}, u32[]{:S(2)}) async-start(f16[4,104,512]{2,1,0:T(8,128)(2,1)} %broadcast_in_dim.51), calls=%async_computation.6 | async-start | bytes 851968 | tf_op jit(solution)/shard_map/all_to_all | solution.py:18
  161.1 1.3 copy-start.7
  164.2 12.2 %all-to-all-start.8 = ((f16[4,200,384]{2,1,0:T(8,128)(2,1)}), f16[4,200,384]{2,1,0:T(8,128)(2,1)S(1)}, u32[]{:S(2)}, u32[]{:S(2)}) async-start(f16[4,200,384]{2,1,0:T(8,128)(2,1)} %pad_maximum_fusion.3), calls=%async_computation.8 | async-start | bytes 1228800 | tf_op jit(solution)/shard_map/all_to_all | solution.py:18
  176.5 0.9 copy-start.2
  176.5 1.7 copy-start
